TPU v7x, 128 devices: a whole 4x4x4 slice. The times are simulated.
128 devices in a mesh: section: 2 (over core), dp: 64 (over x, z, y).
Axes of the slice: x: 4, y: 4, z: 4, core: 2. Of those that a mesh axis runs over, the one named last changes fastest.
Arguments:
- frames: bfloat16 [131072, 512], P('dp'), may hold values from -6 to 6
- cotangent: bfloat16 [131072, 512], P('dp'), may hold values from -6 to 6
- lengths: int32 [256, 4], P('dp'), may hold values from 1 to 256, 512 in all within a row
- bw_ids: int32 [256, 4], P('dp'), may hold values from 0 to 3
- conv_weight: float32 [2, 7, 512], P('section'), may hold values from -2 to 2
- conv_bias: float32 [2, 512], P('section'), may hold values from -4 to 4
- scale_table: float32 [2, 4, 512], P('section'), may hold values from 0.1 to 1.9
- shift_table: float32 [2, 4, 512], P('section'), may hold values from -3 to 3
- w_up: bfloat16 [2, 512, 1536], P('section'), may hold values from -0.25 to 0.25
- b_up: float32 [2, 1536], P('section'), may hold values from -3 to 3
- w_down: bfloat16 [2, 1536, 512], P('section'), may hold values from -0.15625 to 0.15625
- b_down: float32 [2, 512], P('section'), may hold values from -3 to 3
- layer_scale: float32 [2, 512], P('section'), may hold values from 0.5 to 1.5
Outputs:
- acts: bfloat16 [2, 131072, 512], P('section', 'dp')
- in_grad: float32 [2, 131072, 512], P('section', 'dp')
- g_conv_weight: float32 [2, 7, 512], P('section')
- g_conv_bias: float32 [2, 512], P('section')
- g_scale_table: float32 [2, 4, 512], P('section')
- g_shift_table: float32 [2, 4, 512], P('section')
- g_w_up: float32 [2, 512, 1536], P('section')
- g_b_up: float32 [2, 1536], P('section')
- g_w_down: float32 [2, 1536, 512], P('section')
- g_b_down: float32 [2, 512], P('section')
- g_layer_scale: float32 [2, 512], P('section')
Inputs may be any that keep to these rules, and one draw needn't show every extreme that they name: Each row holds the lengths of the 4 clips of one micro-batch of one device, in order, summing to 512; the largest of each row is 256.
All inputs are finite; a program needn't handle non-finite values.
Results may differ from a plain program's by a relative error of at most 0.0074.
Values may be sent and summed in bfloat16 or wider, within the bound.
A program may use at most 192 MiB of HBM per device.

v0:
```python
import jax
import jax.numpy as jnp
from jax import lax
from jax.sharding import PartitionSpec as P

BANDS = 4
CLIPS = 4


def passed_along(shard, axis, by):
    devices = lax.axis_size(axis)
    pairs = [(i, i + by) for i in range(devices) if 0 <= i + by < devices]
    return lax.ppermute(shard, axis, pairs)


def frame_tables(row_lengths, row_ids, length):
    ends = jnp.cumsum(row_lengths, axis=-1)
    position = jnp.arange(length, dtype=jnp.int32)
    segment = jnp.sum((position[:, None] >= ends[..., None, :]).astype(jnp.int32), axis=-1)
    seg_hot = (segment[..., None] == jnp.arange(CLIPS, dtype=jnp.int32)).astype(jnp.float32)
    clip_hot = (row_ids[..., None] == jnp.arange(BANDS, dtype=jnp.int32)).astype(jnp.float32)
    band_hot = jnp.einsum("...tc,...ck->...tk", seg_hot, clip_hot, precision=lax.Precision.HIGHEST)
    return (segment, band_hot)


def prepare(inputs, segment, band_hot, taps, conv_b, scale_tab, shift_tab):
    length = inputs.shape[-2]
    lead = inputs.ndim - 2
    padded = jnp.pad(inputs, [(0, 0)] * lead + [(3, 3), (0, 0)])
    seg_pad = jnp.pad(segment, [(0, 0)] * lead + [(3, 3)], constant_values=-1)
    hidden = conv_b + jnp.zeros_like(inputs)
    for offset in range(taps.shape[0]):
        moved = lax.slice_in_dim(padded, offset, offset + length, axis=lead)
        moved_seg = lax.slice_in_dim(seg_pad, offset, offset + length, axis=lead)
        hidden = hidden + jnp.where((moved_seg == segment)[..., None], moved, 0.0) * taps[offset]
    center = hidden - jnp.mean(hidden, axis=-1, keepdims=True)
    spread = jnp.mean(center * center, axis=-1, keepdims=True)
    normed = center * lax.rsqrt(spread + 1e-06)
    scale = jnp.einsum("...tk,kd->...td", band_hot, scale_tab, precision=lax.Precision.HIGHEST)
    shift = jnp.einsum("...tk,kd->...td", band_hot, shift_tab, precision=lax.Precision.HIGHEST)
    return normed * scale + shift


def block_forward(inputs, segment, band_hot, weights):
    taps, conv_b, scale_tab, shift_tab, up_w, up_b, down_w, down_b, gamma = weights
    adapted = prepare(inputs, segment, band_hot, taps, conv_b, scale_tab, shift_tab).astype(
        jnp.bfloat16
    )
    up_val = jnp.dot(adapted, up_w, preferred_element_type=jnp.float32) + up_b
    gelu_val = jax.nn.gelu(up_val, approximate=False).astype(jnp.bfloat16)
    down_val = jnp.dot(gelu_val, down_w, preferred_element_type=jnp.float32) + down_b
    return inputs + gamma * down_val


def block_backward(inputs, upstream, segment, band_hot, weights):
    taps, conv_b, scale_tab, shift_tab, up_w, up_b, down_w, down_b, gamma = weights

    def local_front(values, taps_in, bias_in, scale_in, shift_in):
        return prepare(values, segment, band_hot, taps_in, bias_in, scale_in, shift_in)

    adapted_f, front_pull = jax.vjp(local_front, inputs, taps, conv_b, scale_tab, shift_tab)
    adapted = adapted_f.astype(jnp.bfloat16)
    up_val = jnp.dot(adapted, up_w, preferred_element_type=jnp.float32) + up_b
    gelu_f, gelu_pull = jax.vjp(lambda value: jax.nn.gelu(value, approximate=False), up_val)
    gelu_val = gelu_f.astype(jnp.bfloat16)
    down_val = jnp.dot(gelu_val, down_w, preferred_element_type=jnp.float32) + down_b
    grad_gamma = jnp.sum(upstream * down_val, axis=0)
    grad_down = (gamma * upstream).astype(jnp.bfloat16)
    grad_wdown = lax.dot_general(
        gelu_val, grad_down, (((0,), (0,)), ((), ())), preferred_element_type=jnp.float32
    )
    grad_bdown = jnp.sum(grad_down.astype(jnp.float32), axis=0)
    grad_gelu = lax.dot_general(
        grad_down, down_w, (((1,), (1,)), ((), ())), preferred_element_type=jnp.float32
    )
    grad_up = gelu_pull(grad_gelu)[0].astype(jnp.bfloat16)
    grad_wup = lax.dot_general(
        adapted, grad_up, (((0,), (0,)), ((), ())), preferred_element_type=jnp.float32
    )
    grad_bup = jnp.sum(grad_up.astype(jnp.float32), axis=0)
    grad_adapt = lax.dot_general(
        grad_up, up_w, (((1,), (1,)), ((), ())), preferred_element_type=jnp.float32
    )
    grad_in, grad_taps, grad_bias, grad_scale, grad_shift = front_pull(grad_adapt)
    parts = (
        grad_taps,
        grad_bias,
        grad_scale,
        grad_shift,
        grad_wup,
        grad_bup,
        grad_wdown,
        grad_bdown,
        grad_gamma,
    )
    return (grad_in + upstream, parts)


def shards(
    frames,
    cotangent,
    lengths,
    bw_ids,
    conv_weight,
    conv_bias,
    scale_table,
    shift_table,
    w_up,
    b_up,
    w_down,
    b_down,
    layer_scale,
):
    steps_count = lengths.shape[0]
    width = frames.shape[1]
    span = frames.shape[0] // steps_count
    first_section = lax.axis_index("section") == 0
    weights = (
        conv_weight[0],
        conv_bias[0],
        scale_table[0],
        shift_table[0],
        w_up[0],
        b_up[0],
        w_down[0],
        b_down[0],
        layer_scale[0],
    )
    inputs_all = frames.reshape(steps_count, span, width).astype(jnp.float32)
    cot_all = cotangent.reshape(steps_count, span, width).astype(jnp.float32)
    received = jnp.zeros((span, width), jnp.bfloat16)
    seen_in = []
    seen_out = []
    for moment in range(steps_count + 1):
        early_step = min(moment, steps_count - 1)
        late_step = max(moment - 1, 0)
        block_in = jnp.where(first_section, inputs_all[early_step], received.astype(jnp.float32))
        segment, band_hot = frame_tables(
            jnp.where(first_section, lengths[early_step], lengths[late_step]),
            jnp.where(first_section, bw_ids[early_step], bw_ids[late_step]),
            span,
        )
        result = block_forward(block_in, segment, band_hot, weights)
        seen_in.append(block_in)
        seen_out.append(result)
        if moment < steps_count:
            received = passed_along(result.astype(jnp.bfloat16), "section", 1)
    acts_rows = [
        jnp.where(first_section, seen_out[index], seen_out[index + 1])
        for index in range(steps_count)
    ]
    acts = jnp.concatenate(acts_rows, axis=0).astype(jnp.bfloat16)[None]
    kept_in = [
        jnp.where(first_section, seen_in[index], seen_in[index + 1]) for index in range(steps_count)
    ]
    totals = tuple((jnp.zeros(w.shape, jnp.float32) for w in weights))
    received_grad = jnp.zeros((span, width), jnp.bfloat16)
    grad_rows = []
    for moment in range(steps_count + 1):
        early_step = min(moment, steps_count - 1)
        late_step = max(moment - 1, 0)
        block_in = jnp.where(first_section, kept_in[late_step], kept_in[early_step])
        upstream = jnp.where(first_section, received_grad.astype(jnp.float32), cot_all[early_step])
        segment, band_hot = frame_tables(
            jnp.where(first_section, lengths[late_step], lengths[early_step]),
            jnp.where(first_section, bw_ids[late_step], bw_ids[early_step]),
            span,
        )
        live = jnp.where(
            first_section,
            jnp.float32(1.0 if moment >= 1 else 0.0),
            jnp.float32(1.0 if moment < steps_count else 0.0),
        )
        grad_in, parts = block_backward(block_in, upstream, segment, band_hot, weights)
        parts = tuple((piece * live for piece in parts))
        totals = tuple((total + piece for total, piece in zip(totals, parts)))
        grad_rows.append(grad_in)
        if moment < steps_count:
            received_grad = passed_along(grad_in.astype(jnp.bfloat16), "section", -1)
    totals = lax.psum(totals, "dp")
    grad_list = [
        jnp.where(
            first_section,
            grad_rows[index + 1],
            grad_rows[index].astype(jnp.bfloat16).astype(jnp.float32),
        )
        for index in range(steps_count)
    ]
    in_grad = jnp.concatenate(grad_list, axis=0)[None]
    outs = tuple((total[None] for total in totals))
    return (
        acts,
        in_grad,
        outs[0],
        outs[1],
        outs[2],
        outs[3],
        outs[4],
        outs[5],
        outs[6],
        outs[7],
        outs[8],
    )


def solution(mesh):
    in_specs = (
        P("dp", None),
        P("dp", None),
        P("dp", None),
        P("dp", None),
        P("section", None, None),
        P("section", None),
        P("section", None, None),
        P("section", None, None),
        P("section", None, None),
        P("section", None),
        P("section", None, None),
        P("section", None),
        P("section", None),
    )
    out_specs = (
        P("section", "dp", None),
        P("section", "dp", None),
        P("section", None, None),
        P("section", None),
        P("section", None, None),
        P("section", None, None),
        P("section", None, None),
        P("section", None),
        P("section", None, None),
        P("section", None),
        P("section", None),
    )
    return jax.shard_map(shards, mesh=mesh, in_specs=in_specs, out_specs=out_specs, check_vma=False)
```

profile of v0, /device:TPU:0, one launch (start us, length us, event | category | flops | bytes accessed | tf_op | source)
XLA Modules:
  0.0 682.3 jit_solution(1262163037971805949)
XLA Ops:
  12.2 2.7 fusion.366
  21.7 10.4 %fusion.219 = bf16[512,512]{1,0:T(8,128)(2,1)S(1)} fusion(f32[512,512]{1,0:T(8,128)} %copy-done.66, bf16[1,1536,512]{2,1,0:T(8,128)(2,1)} %param.23, bf16[1,512,1536]{2,1,0:T(8,128)(2,1)S(1)} %copy-done, f32[1536]{0:T(1024)S(1)} %reduce, f32[512,512]{1,0:T(8,128)} %fusion.366, f32[512,512]{1,0:T(8,128)S(1)} %fusion.379, f32[512,512]{1,0:T(8,128)} %copy-done.67, ...), kind=kOutput, calls=%fused_computation.300 | convolution fusion | flops 1664876544 | bytes 7878656 | tf_op jit(solution)/shard_map/dot_general | solution.py:51
  32.1 2.5 collective-permute-start
  42.0 2.1 fusion.368
  49.8 10.2 %fusion.216 = bf16[512,512]{1,0:T(8,128)(2,1)} fusion(f32[512,512]{1,0:T(8,128)S(1)} %slice_select_fusion.4, bf16[1,1536,512]{2,1,0:T(8,128)(2,1)} %param.23, bf16[512,512]{1,0:T(8,128)(2,1)S(1)} %fusion.225, bf16[1,512,1536]{2,1,0:T(8,128)(2,1)S(1)} %copy-done, f32[1536]{0:T(1024)S(1)} %reduce, f32[512]{0:T(512)S(1)} %bitcast.577, f32[512]{0:T(512)S(1)} %bitcast.520), kind=kOutput, calls=%fused_computation.299 | convolution fusion | flops 1663565824 | bytes 5253120 | tf_op jit(solution)/shard_map/dot_general | solution.py:51
  61.6 2.3 convert_element_type.293
  64.0 2.3 fusion.372
  72.1 8.8 %multiply_convert_fusion.4 = (bf16[512,1536]{1,0:T(8,128)(2,1)}, f32[512,1536]{1,0:T(8,128)S(1)}, f32[512,1536]{1,0:T(8,128)S(1)}) fusion(f32[1536]{0:T(1024)S(1)} %reduce, bf16[512,512]{1,0:T(8,128)(2,1)S(1)} %add_convert_fusion.6, bf16[1,512,1536]{2,1,0:T(8,128)(2,1)S(1)} %copy-done), kind=kOutput, calls=%fused_computation.59 | convolution fusion | flops 857210880 | bytes 9967616 | tf_op jit(solution)/shard_map/dot_general | solution.py:63
  80.9 2.5 convert_reduce_fusion.4
  84.6 2.7 convolution_multiply_fusion.3
  88.5 3.9 multiply_reduce_fusion.34
  92.4 2.4 multiply_select_fusion.29
  99.2 10.2 %fusion.213 = bf16[512,512]{1,0:T(8,128)(2,1)} fusion(f32[512,512]{1,0:T(8,128)S(1)} %copy-done.35, bf16[1,1536,512]{2,1,0:T(8,128)(2,1)} %param.23, bf16[512,512]{1,0:T(8,128)(2,1)S(1)} %fusion.226, bf16[1,512,1536]{2,1,0:T(8,128)(2,1)S(1)} %copy-done, f32[1536]{0:T(1024)S(1)} %reduce, f32[512]{0:T(512)S(1)} %bitcast.578, f32[512]{0:T(512)S(1)} %bitcast.522), kind=kOutput, calls=%fused_computation.298 | convolution fusion | flops 1663565824 | bytes 5253120 | tf_op jit(solution)/shard_map/dot_general | solution.py:51
  110.8 6.2 fusion.619
  117.3 4.9 convolution_multiply_fusion.1
  127.2 9.4 %multiply_convert_fusion.3 = (bf16[512,1536]{1,0:T(8,128)(2,1)}, f32[512,1536]{1,0:T(8,128)}, f32[512,1536]{1,0:T(8,128)}) fusion(f32[1536]{0:T(1024)S(1)} %reduce, bf16[512,512]{1,0:T(8,128)(2,1)S(1)} %fusion.228, bf16[1,512,1536]{2,1,0:T(8,128)(2,1)S(1)} %copy-done), kind=kOutput, calls=%fused_computation.58 | convolution fusion | flops 857210880 | bytes 9967616 | tf_op jit(solution)/shard_map/dot_general | solution.py:63
  138.8 2.6 broadcast_select_fusion.2
  146.6 10.7 %fusion.210 = bf16[512,512]{1,0:T(8,128)(2,1)} fusion(f32[512,512]{1,0:T(8,128)} %copy-done.42, bf16[1,1536,512]{2,1,0:T(8,128)(2,1)} %param.23, bf16[512,512]{1,0:T(8,128)(2,1)} %fusion.227, bf16[1,512,1536]{2,1,0:T(8,128)(2,1)S(1)} %copy-done, f32[1536]{0:T(1024)S(1)} %reduce, f32[512]{0:T(512)S(1)} %bitcast.580, f32[512]{0:T(512)S(1)} %bitcast.524), kind=kOutput, calls=%fused_computation.297 | convolution fusion | flops 1663565824 | bytes 5253120 | tf_op jit(solution)/shard_map/dot_general | solution.py:51
  157.3 4.3 collective-permute-start.3
  161.6 2.6 fusion.316
  164.2 2.2 convert_reduce_fusion.8
  166.3 4.5 convert_reduce_fusion.3
  173.2 2.6 multiply_reduce_fusion.27
  180.4 3.5 convert_select_fusion.4
  186.4 9.4 %multiply_convert_fusion.2 = (bf16[512,1536]{1,0:T(8,128)(2,1)}, f32[512,1536]{1,0:T(8,128)S(1)}, f32[512,1536]{1,0:T(8,128)S(1)}) fusion(f32[1536]{0:T(1024)S(1)} %reduce, bf16[512,512]{1,0:T(8,128)(2,1)S(1)} %fusion.229, bf16[1,512,1536]{2,1,0:T(8,128)(2,1)S(1)} %copy-done), kind=kOutput, calls=%fused_computation.57 | convolution fusion | flops 857210880 | bytes 9967616 | tf_op jit(solution)/shard_map/dot_general | solution.py:63
  195.7 2.8 convolution_add_fusion.2
  198.5 2.2 fusion.240
  201.3 2.7 convolution_add_fusion.5
  214.8 3.6 fusion.622
  219.0 2.2 add_convert_fusion.5
  221.1 9.4 %multiply_convert_fusion = (bf16[512,1536]{1,0:T(8,128)(2,1)}, f32[512,1536]{1,0:T(8,128)}, f32[512,1536]{1,0:T(8,128)}) fusion(f32[1536]{0:T(1024)S(1)} %reduce, bf16[512,512]{1,0:T(8,128)(2,1)S(1)} %get-tuple-element.234, bf16[1,512,1536]{2,1,0:T(8,128)(2,1)S(1)} %copy-done), kind=kOutput, calls=%fused_computation.55 | convolution fusion | flops 857210880 | bytes 9967616 | tf_op jit(solution)/shard_map/dot_general | solution.py:63
  230.5 2.4 convert_select_fusion.3
  235.4 9.4 %multiply_convert_fusion.1 = (bf16[512,1536]{1,0:T(8,128)(2,1)}, f32[512,1536]{1,0:T(8,128)}, f32[512,1536]{1,0:T(8,128)}) fusion(f32[1536]{0:T(1024)S(1)} %reduce, bf16[512,512]{1,0:T(8,128)(2,1)S(1)} %fusion.230, bf16[1,512,1536]{2,1,0:T(8,128)(2,1)S(1)} %copy-done), kind=kOutput, calls=%fused_computation.56 | convolution fusion | flops 857210880 | bytes 9967616 | tf_op jit(solution)/shard_map/dot_general | solution.py:63
  244.9 11.7 %fusion.246 = bf16[1,512,512]{2,1,0:T(8,128)(2,1)} fusion(bf16[512,512]{1,0:T(8,128)(2,1)} %fusion.210, f32[512,512]{1,0:T(8,128)} %copy-done.61, bf16[1,1536,512]{2,1,0:T(8,128)(2,1)} %param.23, bf16[1,512,1536]{2,1,0:T(8,128)(2,1)S(1)} %copy-done, f32[1536]{0:T(1024)S(1)} %reduce, f32[512,512]{1,0:T(8,128)} %get-tuple-element.235, ...), kind=kOutput, calls=%fused_computation.313 | convolution fusion | flops 1664876544 | bytes 8402945 | tf_op jit(solution)/shard_map/dot_general | solution.py:51
  256.6 3.5 convolution_add_fusion.4
  262.6 2.1 convert_reduce_fusion.6
  269.8 2.2 multiply_reduce_fusion.13
  272.4 3.5 convert_select_fusion.1
  283.4 2.7 fusion.3
  286.1 2.7 fusion.2
  291.5 3.0 pad_maximum_fusion
  295.4 2.5 fusion.237
  299.9 2.2 fusion.234
  304.8 3.5 multiply_reduce_fusion.6
  311.1 351.4 %all-reduce.88 = (f32[1,7,512]{2,0,1:T(1,128)}, f32[1,512]{1,0:T(1,128)}, f32[1,4,512]{2,1,0:T(4,128)}, f32[1,4,512]{2,1,0:T(4,128)}, f32[1,1536]{1,0:T(1,128)}, /*index=5*/f32[1,512]{1,0:T(1,128)}, f32[1,512]{1,0:T(1,128)}) all-reduce(f32[1,7,512]{2,0,1:T(1,128)S(1)} %broadcast_in_dim.725, ...), channel_id=1, replica_groups=mesh['section'=2,'dp'=64] {'dp'}, use_global_device_ids=true, to_apply=%region_81.82 | all-reduce | flops 10752 | bytes 86016 | tf_op jit(solution)/shard_map/psum | solution.py:180
  664.4 2.5 fusion.262
  667.0 2.5 maximum_bitcast_fusion
  669.5 3.9 copy.26
  (464 shorter events, 105.6 us)
Async XLA Ops:
  7.2 14.5 %copy-start = (bf16[1,512,1536]{2,1,0:T(8,128)(2,1)S(1)}, bf16[1,512,1536]{2,1,0:T(8,128)(2,1)}, u32[]{:S(2)}) copy-start(bf16[1,512,1536]{2,1,0:T(8,128)(2,1)} %param.21) | copy-start | bytes 4718596
  7.2 662.3 %all-reduce.92.cloned.1.call-start = ((), (), s32[]{:S(2)}) async-start(), calls=%async_computation | async-start | bytes 12582912 | tf_op jit(solution)/shard_map/psum | solution.py:180
  9.1 5.9 copy-start.82
  12.2 9.4 %copy-start.32 = (f32[512,512]{1,0:T(8,128)}, f32[512,512]{1,0:T(8,128)S(1)}, u32[]{:S(2)}) copy-start(f32[512,512]{1,0:T(8,128)S(1)} %fusion.379) | copy-start | bytes 3145732
  21.7 12.9 %copy-start.131 = (s32[4,4]{1,0:T(4,128)S(1)}, s32[4,4]{1,0:T(4,128)}, u32[]{:S(2)}) copy-start(s32[4,4]{1,0:T(4,128)} %param.16) | copy-start | bytes 196
  21.7 18.3 %copy-start.93 = (f32[1,4,512]{2,1,0:T(4,128)S(1)}, f32[1,4,512]{2,1,0:T(4,128)}, u32[]{:S(2)}) copy-start(f32[1,4,512]{2,1,0:T(4,128)} %param.19) | copy-start | bytes 24580
  32.1 15.2 %copy-start.95 = (bf16[512,512]{1,0:T(8,128)(2,1)}, bf16[512,512]{1,0:T(8,128)(2,1)S(1)}, u32[]{:S(2)}) copy-start(bf16[512,512]{1,0:T(8,128)(2,1)S(1)} %fusion.219) | copy-start | bytes 1572868
  32.1 11.9 %collective-permute-start = (bf16[512,512]{1,0:T(8,128)(2,1)S(1)}, bf16[512,512]{1,0:T(8,128)(2,1)}, u32[]{:S(2)}, u32[]{:S(2)}) collective-permute-start(bf16[512,512]{1,0:T(8,128)(2,1)S(1)} %fusion.219), channel_id=1, source_target_pairs={{0,64},{1,65},{2,66},{3,67},{4,68},{5,69},{6,70},{7,71},{8,72},{9,... | collective-permute-start | bytes 1572872 | tf_op jit(solution)/shard_map/ppermute | solution.py:13
  38.5 5.5 copy-start.97
  38.8 5.2 copy-start.99
  39.6 145.5 %copy-start.101 = (f32[512,4]{0,1:T(4,128)}, f32[512,4]{0,1:T(4,128)S(1)}, u32[]{:S(2)}) copy-start(f32[512,4]{0,1:T(4,128)S(1)} %fusion.348) | copy-start | bytes 24580
  45.6 22.7 %copy-start.26 = (f32[512,512]{1,0:T(8,128)}, f32[512,512]{1,0:T(8,128)S(1)}, u32[]{:S(2)}) copy-start(f32[512,512]{1,0:T(8,128)S(1)} %slice_select_fusion.4) | copy-start | bytes 3145732
  60.0 8.3 %collective-permute-start.1 = (bf16[512,512]{1,0:T(8,128)(2,1)}, bf16[512,512]{1,0:T(8,128)(2,1)S(1)}, u32[]{:S(2)}, u32[]{:S(2)}) collective-permute-start(bf16[512,512]{1,0:T(8,128)(2,1)} %fusion.216), channel_id=1, source_target_pairs={{0,64},{1,65},{2,66},{3,67},{4,68},{5,69},{6,70},{7,71},{8,72},{9,... | collective-permute-start | bytes 1572872 | tf_op jit(solution)/shard_map/ppermute | solution.py:13
  61.6 6.7 copy-start.15
  63.9 17.0 %copy-start.1 = (f32[2048,512]{1,0:T(8,128)}, f32[2048,512]{1,0:T(8,128)S(1)}, u32[]{:S(2)}) copy-start(f32[2048,512]{1,0:T(8,128)S(1)} %convert_element_type.293) | copy-start | bytes 12582916
  69.8 25.0 %copy-start.34 = (f32[512,512]{1,0:T(8,128)}, f32[512,512]{1,0:T(8,128)S(1)}, u32[]{:S(2)}) copy-start(f32[512,512]{1,0:T(8,128)S(1)} %get-tuple-element.100) | copy-start | bytes 3145732
  72.1 8.9 %copy-start.139 = (bf16[1,1536,512]{2,1,0:T(8,128)(2,1)S(1)}, bf16[1,1536,512]{2,1,0:T(8,128)(2,1)}, u32[]{:S(2)}) copy-start(bf16[1,1536,512]{2,1,0:T(8,128)(2,1)} %param.23) | copy-start | bytes 4718596
  109.4 29.4 %collective-permute-start.2 = (bf16[512,512]{1,0:T(8,128)(2,1)}, bf16[512,512]{1,0:T(8,128)(2,1)S(1)}, u32[]{:S(2)}, u32[]{:S(2)}) collective-permute-start(bf16[512,512]{1,0:T(8,128)(2,1)} %fusion.213), channel_id=1, source_target_pairs={{0,64},{1,65},{2,66},{3,67},{4,68},{5,69},{6,70},{7,71},{8,72},{9,... | collective-permute-start | bytes 1572872 | tf_op jit(solution)/shard_map/ppermute | solution.py:13
  110.7 11.4 %copy-start.64 = (f32[512,512]{1,0:T(8,128)S(1)}, f32[512,512]{1,0:T(8,128)}, u32[]{:S(2)}) copy-start(f32[512,512]{1,0:T(8,128)} %get-tuple-element.156) | copy-start | bytes 3145732
  110.7 11.4 %copy-start.65 = (f32[512,512]{1,0:T(8,128)S(1)}, f32[512,512]{1,0:T(8,128)}, u32[]{:S(2)}) copy-start(f32[512,512]{1,0:T(8,128)} %get-tuple-element.157) | copy-start | bytes 3145732
  116.9 55.0 %copy-start.10 = (f32[512,512]{1,0:T(8,128)}, f32[512,512]{1,0:T(8,128)S(1)}, u32[]{:S(2)}) copy-start(f32[512,512]{1,0:T(8,128)S(1)} %get-tuple-element.97) | copy-start | bytes 3145732
  117.0 5.2 copy-start.63
  117.3 5.6 copy-start.62
  124.7 39.4 %collective-permute-start.4 = (bf16[512,512]{1,0:T(8,128)(2,1)}, bf16[512,512]{1,0:T(8,128)(2,1)}, u32[]{:S(2)}, u32[]{:S(2)}) collective-permute-start(bf16[512,512]{1,0:T(8,128)(2,1)} %fusion.267), channel_id=1, source_target_pairs={{64,0},{65,1},{66,2},{67,3},{68,4},{69,5},{70,6},{71,7},{72,8},{73... | collective-permute-start | bytes 1572872 | tf_op jit(solution)/shard_map/ppermute | solution.py:13
  127.2 9.4 %copy-start.23 = (f32[512,512]{1,0:T(8,128)S(1)}, f32[512,512]{1,0:T(8,128)}, u32[]{:S(2)}) copy-start(f32[512,512]{1,0:T(8,128)} %copy-done.22) | copy-start | bytes 3145732
  127.2 10.0 %copy-start.140 = (bf16[1,1536,512]{2,1,0:T(8,128)(2,1)S(1)}, bf16[1,1536,512]{2,1,0:T(8,128)(2,1)}, u32[]{:S(2)}) copy-start(bf16[1,1536,512]{2,1,0:T(8,128)(2,1)} %param.23) | copy-start | bytes 4718596
  127.2 10.0 %copy-start.145 = (bf16[512,1536]{1,0:T(8,128)(2,1)S(1)}, bf16[512,1536]{1,0:T(8,128)(2,1)}, u32[]{:S(2)}) copy-start(bf16[512,1536]{1,0:T(8,128)(2,1)} %get-tuple-element.60) | copy-start | bytes 4718596
  157.3 9.1 %copy-start.141 = (bf16[1,1536,512]{2,1,0:T(8,128)(2,1)S(1)}, bf16[1,1536,512]{2,1,0:T(8,128)(2,1)}, u32[]{:S(2)}) copy-start(bf16[1,1536,512]{2,1,0:T(8,128)(2,1)} %param.23) | copy-start | bytes 4718596
  157.3 9.1 %copy-start.148 = (f32[512,1536]{1,0:T(8,128)S(1)}, f32[512,1536]{1,0:T(8,128)}, u32[]{:S(2)}) copy-start(f32[512,1536]{1,0:T(8,128)} %get-tuple-element.63) | copy-start | bytes 9437188
  157.3 53.6 %collective-permute-start.3 = (bf16[512,512]{1,0:T(8,128)(2,1)}, bf16[512,512]{1,0:T(8,128)(2,1)S(1)}, u32[]{:S(2)}, u32[]{:S(2)}) collective-permute-start(bf16[512,512]{1,0:T(8,128)(2,1)} %fusion.210), channel_id=1, source_target_pairs={{0,64},{1,65},{2,66},{3,67},{4,68},{5,69},{6,70},{7,71},{8,72},{9,... | collective-permute-start | bytes 1572872 | tf_op jit(solution)/shard_map/ppermute | solution.py:13
  183.8 20.2 %collective-permute-start.5 = (bf16[512,512]{1,0:T(8,128)(2,1)S(1)}, bf16[512,512]{1,0:T(8,128)(2,1)S(1)}, u32[]{:S(2)}, u32[]{:S(2)}) collective-permute-start(bf16[512,512]{1,0:T(8,128)(2,1)S(1)} %get-tuple-element.79), channel_id=1, source_target_pairs={{64,0},{65,1},{66,2},{67,3},{68,4},{69,5},{70,6},{71,7},{72,8},{73... | collective-permute-start | bytes 1572872 | tf_op jit(solution)/shard_map/ppermute | solution.py:13
  186.3 9.4 %copy-start.75 = (bf16[512,512]{1,0:T(8,128)(2,1)}, bf16[512,512]{1,0:T(8,128)(2,1)S(1)}, u32[]{:S(2)}) copy-start(bf16[512,512]{1,0:T(8,128)(2,1)S(1)} %fusion.229) | copy-start | bytes 1572868
  186.3 9.4 %copy-start.38 = (f32[1536,512]{1,0:T(8,128)S(1)}, f32[1536,512]{1,0:T(8,128)}, u32[]{:S(2)}) copy-start(f32[1536,512]{1,0:T(8,128)} %convolution_multiply_fusion.1) | copy-start | bytes 9437188
  186.4 9.4 %copy-start.54 = (bf16[512,1536]{1,0:T(8,128)(2,1)S(1)}, bf16[512,1536]{1,0:T(8,128)(2,1)}, u32[]{:S(2)}) copy-start(bf16[512,1536]{1,0:T(8,128)(2,1)} %get-tuple-element.62) | copy-start | bytes 4718596
  204.1 26.5 %copy-start.83 = (bf16[512,512]{1,0:T(8,128)(2,1)}, bf16[512,512]{1,0:T(8,128)(2,1)S(1)}, u32[]{:S(2)}) copy-start(bf16[512,512]{1,0:T(8,128)(2,1)S(1)} %collective-permute-done.5) | copy-start | bytes 1572868
  212.5 5.8 copy-start.39
  212.6 5.8 copy-start.61
  214.4 19.8 %copy-start.7 = (f32[512,512]{1,0:T(8,128)}, f32[512,512]{1,0:T(8,128)S(1)}, u32[]{:S(2)}) copy-start(f32[512,512]{1,0:T(8,128)S(1)} %get-tuple-element.106) | copy-start | bytes 3145732
  218.4 12.1 %copy-start.12 = (f32[512,512]{1,0:T(8,128)}, f32[512,512]{1,0:T(8,128)S(1)}, u32[]{:S(2)}) copy-start(f32[512,512]{1,0:T(8,128)S(1)} %get-tuple-element.111) | copy-start | bytes 3145732
  218.4 12.1 %copy-start.57 = (f32[512,512]{1,0:T(8,128)}, f32[512,512]{1,0:T(8,128)S(1)}, u32[]{:S(2)}) copy-start(f32[512,512]{1,0:T(8,128)S(1)} %get-tuple-element.162) | copy-start | bytes 3145732
  221.1 9.4 %copy-start.79 = (bf16[512,512]{1,0:T(8,128)(2,1)}, bf16[512,512]{1,0:T(8,128)(2,1)S(1)}, u32[]{:S(2)}) copy-start(bf16[512,512]{1,0:T(8,128)(2,1)S(1)} %get-tuple-element.234) | copy-start | bytes 1572868
  232.9 28.6 %collective-permute-start.6 = (bf16[512,512]{1,0:T(8,128)(2,1)}, bf16[512,512]{1,0:T(8,128)(2,1)}, u32[]{:S(2)}, u32[]{:S(2)}) collective-permute-start(bf16[512,512]{1,0:T(8,128)(2,1)} %get-tuple-element.81), channel_id=1, source_target_pairs={{64,0},{65,1},{66,2},{67,3},{68,4},{69,5},{70,6},{71,7},{72,8},{73... | collective-permute-start | bytes 1572872 | tf_op jit(solution)/shard_map/ppermute | solution.py:13
  235.4 9.4 %copy-start.77 = (bf16[512,512]{1,0:T(8,128)(2,1)}, bf16[512,512]{1,0:T(8,128)(2,1)S(1)}, u32[]{:S(2)}) copy-start(bf16[512,512]{1,0:T(8,128)(2,1)S(1)} %fusion.230) | copy-start | bytes 1572868
  244.9 11.7 %copy-start.76 = (bf16[512,512]{1,0:T(8,128)(2,1)S(1)}, bf16[512,512]{1,0:T(8,128)(2,1)}, u32[]{:S(2)}) copy-start(bf16[512,512]{1,0:T(8,128)(2,1)} %copy-done.75) | copy-start | bytes 1572868
  275.9 4.7 collective-permute-start.7
  304.8 5.2 copy-start.56
  304.8 5.2 copy-start.91
  311.0 351.8 %copy-start.89 = (bf16[512,512]{1,0:T(8,128)(2,1)S(1)}, bf16[512,512]{1,0:T(8,128)(2,1)}, u32[]{:S(2)}) copy-start(bf16[512,512]{1,0:T(8,128)(2,1)} %copy-done.88) | copy-start | bytes 1572868
  (112 other events, 331.7 us)
Sparse Core Ops, SparseCore 0:
  289.0 152.7 all-reduce.91
where the time goes:
time: 692 us; the launch traced here: 682 us
  blocking collectives  351 us (51%)
  matrix products  189 us (27%)
  other arithmetic  87 us (13%)
  local copies, waits for them, and re-layouts  22 us (3%)
  between operations  16.6 us (2%)
  starting transfers between devices  14.9 us (2%)
    psum x1, blocking collectives, shards(): totals = lax.psum(totals, 'dp')  351 us
    dot_general x5, matrix products, block_forward(): jnp.dot(gelu_val, down_w, preferred_element_type=jnp.float32) + down_b  53.2 us
    dot_general x5, matrix products, block_backward(): up_val = jnp.dot(adapted, up_w, preferred_element_type=jnp.float32) + up_b  46.3 us
    reduce_sum x14, other arithmetic, prepare(): center = hidden - jnp.mean(hidden, axis=-1, keepdims=True)  24.1 us
    unnamed x304, local copies, waits for them, and re-layouts  20.2 us
    dot_general x13, matrix products, prepare(): jnp.einsum('...tk,kd->...td', band_hot, scale_tab, precision=lax.Precisio...  18.1 us
    dot_general x13, matrix products, prepare(): jnp.einsum('...tk,kd->...td', band_hot, shift_tab, precision=lax.Precisio...  16.8 us
    ppermute x8, starting transfers between devices, passed_along(): return lax.ppermute(shard, axis, pairs)  14.8 us
  transfers between devices with their start and end apart: 9, of which 1 were waited for; matrix products, arithmetic and copies ran while one was open for 23% of the time, Pallas kernels for 0%

commit v1 on v0

v1 whole, which is shorter than its diff:
```python
import functools
import math

import jax
import jax.numpy as jnp
import numpy as np
from jax import lax
from jax.experimental import pallas as pl
from jax.experimental.pallas import tpu as pltpu
from jax.sharding import PartitionSpec as P

BF = jnp.bfloat16
F32 = jnp.float32
MESH = pl.DeviceIdType.MESH
MIB = 2**20

SPAN = 512
D = 512
FF = 1536
ROWS = 2
M = ROWS * SPAN
HALO = 8
PADDED = SPAN + 2 * HALO
STEP = 64
TILE = 256
GRADS = 2 * FF
SMALL = 32
EXP_SCALE = -0.5 * math.log2(math.e)
PDF_SCALE = 1.0 / math.sqrt(2.0 * math.pi)
ERF_SCALE = 1.0 / math.sqrt(2.0)
TAPS, CBIAS, SCALE, SHIFT, DBIAS, GAMMA, UBIAS = 0, 7, 8, 12, 16, 17, 18
SMALL_ROWS = 21
OFFSETS = (0, 1, 2, 4, 5, 6)


def at(start, size):
    return slice(start, start + size) if isinstance(start, int) else pl.ds(start, size)


def times(index, size):
    return index * size if isinstance(index, int) else pl.multiple_of(index * size, size)


def over_rows(value):
    return jnp.sum(value.reshape(value.shape[0] // 8, 8, value.shape[1]), axis=0)


def dot(a, b, dims):
    return lax.dot_general(a, b, (dims, ((), ())), preferred_element_type=F32)


def clip_tables(first, lengths, ids, masks, hot):
    for r in range(ROWS):
        row = first + r
        ends = [lengths[row, 0]]
        for c in (1, 2):
            ends.append(ends[-1] + lengths[row, c])
        band_of = [ids[row, c] for c in range(4)]

        def segment(frame):
            return sum((frame >= end).astype(jnp.int32) for end in ends)

        @pl.loop(0, SPAN // STEP, unroll=2)
        def _(i):
            frame = lax.broadcasted_iota(jnp.int32, (STEP, 128), 0) + i * STEP
            lane = lax.broadcasted_iota(jnp.int32, (STEP, 128), 1)
            here = segment(frame)
            for q, k in enumerate(OFFSETS):
                there = frame + (k - 3)
                same = (segment(there) == here) & (there >= 0) & (there < SPAN)
                masks[r, q, at(times(i, STEP), STEP), :] = jnp.where(same, 1.0, 0.0)
            band = jnp.where(here == 2, band_of[2], band_of[3])
            band = jnp.where(here == 1, band_of[1], band)
            band = jnp.where(here == 0, band_of[0], band)
            one = (lane == band) | (lane == band + 4)
            hot[at(r * SPAN + times(i, STEP), STEP), :] = jnp.where(one, 1.0, 0.0).astype(BF)


def band_table(small, table):
    table[...] = jnp.zeros_like(table)
    for half, first in enumerate((SCALE, SHIFT)):
        whole = small[first : first + 4, :]
        upper = whole.astype(BF).astype(F32)
        both = jnp.concatenate([upper, whole - upper], axis=0)
        table[0:8, half * D : (half + 1) * D] = both.astype(BF)


def conv_norm(x, padded, masks, hot, table, small, normed, rstd_out, adapted):
    for r in range(ROWS):
        for j in range(4):
            padded[r, j, 0:HALO] = jnp.zeros((HALO, 128), F32)
            padded[r, j, HALO + SPAN :] = jnp.zeros((HALO, 128), F32)
            padded[r, j, HALO : HALO + SPAN] = x[r * SPAN : (r + 1) * SPAN, 128 * j : 128 * (j + 1)].astype(F32)

        @pl.loop(0, SPAN // STEP, unroll=8)
        def _(i):
            here = at(times(i, STEP), STEP)
            hidden = []
            for j in range(4):
                c = slice(128 * j, 128 * (j + 1))
                total = small[CBIAS : CBIAS + 1, c] + padded[r, j, at(times(i, STEP) + HALO, STEP), :] * small[3:4, c]
                for q, k in enumerate(OFFSETS):
                    moved = padded[r, j, pl.ds(i * STEP + (HALO + k - 3), STEP), :]
                    total = total + moved * masks[r, q, here, :] * small[k : k + 1, c]
                hidden.append(total)
            mean = jnp.sum(hidden[0] + hidden[1] + hidden[2] + hidden[3], axis=1, keepdims=True) * (1.0 / D)
            center = [h - mean for h in hidden]
            square = [c * c for c in center]
            spread = jnp.sum(square[0] + square[1] + square[2] + square[3], axis=1, keepdims=True) * (1.0 / D)
            rstd = lax.rsqrt(spread + 1e-6)
            rows = at(r * SPAN + times(i, STEP), STEP)
            tables = dot(hot[rows, :], table[...], ((1,), (0,)))
            rstd_out[rows, :] = jnp.broadcast_to(rstd, (STEP, 128))
            for j in range(4):
                c = slice(128 * j, 128 * (j + 1))
                n = center[j] * rstd
                normed[rows, c] = n
                adapted[rows, c] = (n * tables[:, c] + tables[:, D + 128 * j : D + 128 * (j + 1)]).astype(BF)


def up_gelu(adapted, w_up, small, g, slope):
    for i in range(M // TILE):
        rows = at(i * TILE, TILE)
        for c in range(FF // TILE):
            cols = at(c * TILE, TILE)
            bias = small[UBIAS + c // 2 : UBIAS + c // 2 + 1, at((c % 2) * TILE, TILE)]
            u = dot(adapted[rows, :], w_up[:, cols], ((1,), (0,))) + bias
            pdf = jnp.exp2((u * EXP_SCALE) * u) * PDF_SCALE
            cdf = 0.5 + 0.5 * lax.erf(u * ERF_SCALE)
            g[rows, cols] = (u * cdf).astype(BF)
            slope[rows, cols] = (cdf + u * pdf).astype(BF)


def down(x, g, w_down, small, out, upstream, v_out, g_gamma):
    for i in range(M // TILE):
        rows = at(i * TILE, TILE)
        for c in range(2):
            cols = at(c * TILE, TILE)
            v = dot(g[rows, :], w_down[:, cols], ((1,), (0,))) + small[DBIAS : DBIAS + 1, cols]
            out[rows, cols] = (x[rows, cols].astype(F32) + small[GAMMA : GAMMA + 1, cols] * v).astype(BF)
            if v_out is not None:
                v_out[rows, cols] = v.astype(BF)
            if upstream is not None:
                g_gamma[:, cols] += over_rows(upstream[rows, cols].astype(F32) * v)


def down_back(upstream, w_down, small, slope, dv_out, du_out, g_dbias, g_ubias, v, g_gamma):
    for i in range(M // TILE):
        rows = at(i * TILE, TILE)
        dy = upstream[rows, :].astype(F32)
        dv = small[GAMMA : GAMMA + 1, :] * dy
        g_dbias[...] += over_rows(dv)
        if v is not None:
            g_gamma[...] += over_rows(dy * v[rows, :].astype(F32))
        dv = dv.astype(BF)
        dv_out[rows, :] = dv
        for c in range(FF // TILE):
            cols = at(c * TILE, TILE)
            du = dot(dv, w_down[cols, :], ((1,), (1,))) * slope[rows, cols].astype(F32)
            du_out[rows, cols] = du.astype(BF)
            g_ubias[:, cols] += over_rows(du)


def down_grad(g, dv, out):
    for c in range(FF // TILE):
        cols = at(c * TILE, TILE)
        out[cols, :] = dot(g[:, cols], dv[...], ((0,), (0,))).astype(BF)


def up_grad(adapted, du, out):
    for c in range(FF // TILE):
        place = (at(FF + (c // 2) * D, D), at((c % 2) * TILE, TILE))
        out[place] = dot(adapted[...], du[:, at(c * TILE, TILE)], ((0,), (0,))).astype(BF)


def norm_back(du, w_up, hot, table, normed, rstd, d_hidden, g_table):
    half = 512
    for i in range(M // half):
        rows = at(i * half, half)
        da = dot(du[rows, :], w_up[...], ((1,), (1,)))
        n = normed[rows, :]
        dan = da * n
        ones = hot[rows, 0:16]
        g_table[:, 0:D] += dot(ones, dan.astype(BF), ((0,), (0,)))[0:8]
        g_table[:, D:] += dot(ones, da.astype(BF), ((0,), (0,)))[0:8]
        scale = dot(hot[rows, :], table[:, 0:D], ((1,), (0,)))
        dn = da * scale
        mean = jnp.sum(dn, axis=1, keepdims=True) * (1.0 / D)
        along = jnp.sum(dan * scale, axis=1, keepdims=True) * (1.0 / D)
        dh = (dn - mean - n * along) * rstd[rows, 0:1]
        r, first = i * half // SPAN, i * half % SPAN
        for j in range(4):
            d_hidden[r, j, at(HALO + first, half), :] = dh[:, 128 * j : 128 * (j + 1)]


def conv_back(x, upstream, d_hidden, masks, small, g_taps, g_cbias, out):
    for r in range(ROWS):
        for j in range(4):
            d_hidden[r, j, 0:HALO] = jnp.zeros((HALO, 128), F32)
            d_hidden[r, j, HALO + SPAN :] = jnp.zeros((HALO, 128), F32)

        @pl.loop(0, SPAN // STEP, unroll=2)
        def _(i):
            rows = at(r * SPAN + times(i, STEP), STEP)
            here = at(times(i, STEP), STEP)
            for j in range(4):
                c = slice(128 * j, 128 * (j + 1))
                value = x[rows, c].astype(F32)
                dh = d_hidden[r, j, at(times(i, STEP) + HALO, STEP), :]
                total = upstream[rows, c].astype(F32) + dh * small[3:4, c]
                g_cbias[:, c] += over_rows(dh)
                g_taps[3, :, c] += over_rows(value * dh)
                for q, k in enumerate(OFFSETS):
                    part = d_hidden[r, j, pl.ds(i * STEP + (HALO + k - 3), STEP), :] * masks[r, q, here, :]
                    total = total + part * small[6 - k : 7 - k, c]
                    g_taps[6 - k, :, c] += over_rows(value * part)
                out[rows, c] = total.astype(out.dtype)


def small_grads(out, g_taps, g_cbias, g_table, g_dbias, g_gamma, g_ubias):
    def whole(value):
        return jnp.sum(value, axis=0, keepdims=True)

    rows = [whole(g_taps[k]) for k in range(7)] + [whole(g_cbias[...])]
    rows += [g_table[0:4, 0:D], g_table[0:4, D:], whole(g_dbias[...]), whole(g_gamma[...])]
    rows += [whole(g_ubias[:, k * D : (k + 1) * D]) for k in range(3)]
    rows.append(jnp.zeros((SMALL - SMALL_ROWS, D), F32))
    out[...] = jnp.concatenate(rows, axis=0)


def compute_kernel(
    lengths, ids, frames, cotangent, own_small, far_small, own_up, far_up, own_down, far_down,
    acts_out, grad_out, weight_out, small_out,
    x0, cot, small, w_up, w_down, acts, grads, weight_grads, small_sums,
    padded, masks, hot, table, normed, rstd, adapted, g, slope, v0, dv, du, d_hidden,
    g_table, g_taps, g_cbias, g_dbias, g_ubias, g_gamma, in_sems, out_sems,
):
    section = lax.axis_index("section")
    mine = pl.ds(pl.multiple_of(section * M, M), M)
    loads = [
        pltpu.make_async_copy(frames.at[mine], x0, in_sems.at[0]),
        pltpu.make_async_copy(cotangent.at[mine], cot, in_sems.at[1]),
        pltpu.make_async_copy(own_small, small.at[section], in_sems.at[2]),
        pltpu.make_async_copy(far_small, small.at[1 - section], in_sems.at[3]),
        pltpu.make_async_copy(own_up, w_up.at[section], in_sems.at[4]),
        pltpu.make_async_copy(far_up, w_up.at[1 - section], in_sems.at[5]),
        pltpu.make_async_copy(own_down, w_down.at[section], in_sems.at[6]),
        pltpu.make_async_copy(far_down, w_down.at[1 - section], in_sems.at[7]),
    ]
    for load in loads:
        load.start()
    stores = []

    def store(src, dst):
        copy = pltpu.make_async_copy(src, dst, out_sems.at[len(stores)])
        copy.start()
        stores.append(copy)

    clip_tables(section * ROWS, lengths, ids, masks, hot)
    for ref in (g_table, g_taps, g_cbias, g_dbias, g_ubias, g_gamma):
        ref[...] = jnp.zeros_like(ref)
    for i in (0, 2, 3):
        loads[i].wait()
    for b in range(2):
        band_table(small.at[b], table.at[b])
    for b, x in ((0, x0), (1, acts.at[0])):
        conv_norm(x, padded, masks, hot, table.at[b], small.at[b], normed.at[b], rstd.at[b], adapted.at[b])
        if b == 0:
            for i in (4, 5, 6, 7, 1):
                loads[i].wait()
        up_gelu(adapted.at[b], w_up.at[b], small.at[b], g.at[b], slope.at[b])
        if b == 0:
            down(x, g.at[b], w_down.at[b], small.at[b], acts.at[0], None, v0, None)
        else:
            down(x, g.at[b], w_down.at[b], small.at[b], acts.at[1], cot, None, g_gamma.at[1])
        store(acts.at[b], acts_out.at[b])
    for b, x, dy in ((1, acts.at[0], cot), (0, x0, grads.at[1])):
        v = v0 if b == 0 else None
        down_back(
            dy, w_down.at[b], small.at[b], slope.at[b], dv, du, g_dbias.at[b], g_ubias.at[b], v, g_gamma.at[b]
        )
        down_grad(g.at[b], dv, weight_grads.at[b])
        up_grad(adapted.at[b], du, weight_grads.at[b])
        store(weight_grads.at[b], weight_out.at[b])
        norm_back(du, w_up.at[b], hot, table.at[b], normed.at[b], rstd.at[b], d_hidden, g_table.at[b])
        conv_back(x, dy, d_hidden, masks, small.at[b], g_taps.at[b], g_cbias.at[b], grads.at[b])
        store(grads.at[b], grad_out.at[b])
        small_grads(
            small_sums.at[b], g_taps.at[b], g_cbias.at[b], g_table.at[b], g_dbias.at[b], g_gamma.at[b], g_ubias.at[b]
        )
    store(small_sums, small_out)
    for copy in stores:
        copy.wait()


def compute(lengths, ids, *arrays):
    smem = pl.BlockSpec(memory_space=pltpu.SMEM)
    hbm = pl.BlockSpec(memory_space=pl.ANY)
    return pl.pallas_call(
        compute_kernel,
        out_shape=[
            jax.ShapeDtypeStruct((2, M, D), BF),
            jax.ShapeDtypeStruct((2, M, D), BF),
            jax.ShapeDtypeStruct((2, GRADS, D), BF),
            jax.ShapeDtypeStruct((2, SMALL, D), F32),
        ],
        in_specs=[smem, smem] + [hbm] * 8,
        out_specs=[hbm] * 4,
        scratch_shapes=[
            pltpu.VMEM((M, D), BF),
            pltpu.VMEM((M, D), BF),
            pltpu.VMEM((2, 24, D), F32),
            pltpu.VMEM((2, D, FF), BF),
            pltpu.VMEM((2, FF, D), BF),
            pltpu.VMEM((2, M, D), BF),
            pltpu.VMEM((2, M, D), BF),
            pltpu.VMEM((2, GRADS, D), BF),
            pltpu.VMEM((2, SMALL, D), F32),
            pltpu.VMEM((ROWS, 4, PADDED, 128), F32),
            pltpu.VMEM((ROWS, 6, SPAN, 128), F32),
            pltpu.VMEM((M, 128), BF),
            pltpu.VMEM((2, 128, 2 * D), BF),
            pltpu.VMEM((2, M, D), F32),
            pltpu.VMEM((2, M, 128), F32),
            pltpu.VMEM((2, M, D), BF),
            pltpu.VMEM((2, M, FF), BF),
            pltpu.VMEM((2, M, FF), BF),
            pltpu.VMEM((M, D), BF),
            pltpu.VMEM((M, D), BF),
            pltpu.VMEM((M, FF), BF),
            pltpu.VMEM((ROWS, 4, PADDED, 128), F32),
            pltpu.VMEM((2, 8, 2 * D), F32),
            pltpu.VMEM((2, 7, 8, D), F32),
            pltpu.VMEM((2, 8, D), F32),
            pltpu.VMEM((2, 8, D), F32),
            pltpu.VMEM((2, 8, FF), F32),
            pltpu.VMEM((2, 8, D), F32),
            pltpu.SemaphoreType.DMA((8,)),
            pltpu.SemaphoreType.DMA((8,)),
        ],
        compiler_params=pltpu.CompilerParams(vmem_limit_bytes=62 * MIB),
        cost_estimate=pl.CostEstimate(flops=24 * M * D * FF, bytes_accessed=24 * MIB, transcendentals=4 * M * FF),
    )(lengths, ids, *arrays)


PARTS = 3
PART_ROWS = GRADS // PARTS


def reduce_kernel(
    acts, grads, weight_grads, small_sums,
    acts_all, grads_all, weight_all, small_all,
    own, far, pair, got1, got2, got3, sum1, sum2, small_own, small_far, small_pair, small_got, small_sum,
    load_sems, pair_send, pair_recv, send, recv, back_send, back_recv, small_send, small_recv,
):
    section = lax.axis_index("section")
    dp = lax.axis_index("dp")
    coords = (dp // 16, (dp // 4) % 4, dp % 4)
    strides = (16, 4, 1)

    def peer(axis, distance):
        moved = lax.rem(coords[axis] + distance, 4)
        return {"dp": dp + (moved - coords[axis]) * strides[axis], "section": section}

    other = {"dp": dp, "section": 1 - section}

    loads = [
        pltpu.make_async_copy(weight_grads.at[1 - section], far, load_sems.at[0]),
        pltpu.make_async_copy(weight_grads.at[section], own, load_sems.at[1]),
        pltpu.make_async_copy(small_sums.at[1 - section], small_far, load_sems.at[2]),
        pltpu.make_async_copy(small_sums.at[section], small_own, load_sems.at[3]),
        pltpu.make_async_copy(acts.at[section], acts_all.at[pl.ds(pl.multiple_of(section * M, M), M)], load_sems.at[4]),
        pltpu.make_async_copy(grads.at[section], grads_all.at[pl.ds(pl.multiple_of(section * M, M), M)], load_sems.at[5]),
    ]
    for load in loads:
        load.start()

    barrier = pltpu.get_barrier_semaphore()
    pl.semaphore_signal(barrier, inc=1, device_id=other, device_id_type=MESH)
    for axis in range(3):
        for distance in (1, 2, 3):
            pl.semaphore_signal(barrier, inc=1, device_id=peer(axis, distance), device_id_type=MESH)
    pl.semaphore_wait(barrier, 10)

    def copy(src, dst, send_sem, recv_sem, device):
        made = pltpu.make_async_remote_copy(
            src_ref=src, dst_ref=dst, send_sem=send_sem, recv_sem=recv_sem, device_id=device, device_id_type=MESH
        )
        made.start()
        return made

    waits = []
    loads[0].wait()
    pairs = []
    for p in range(PARTS):
        rows = at(p * PART_ROWS, PART_ROWS)
        pairs.append(copy(far.at[rows], pair.at[rows], pair_send.at[p], pair_recv.at[p], other))
    loads[2].wait()
    pairs.append(copy(small_far, small_pair, pair_send.at[3], pair_recv.at[3], other))
    place = pl.ds(pl.multiple_of(section * M, M), M)
    pairs.append(copy(acts.at[1 - section], acts_all.at[place], pair_send.at[4], pair_recv.at[4], other))
    pairs.append(copy(grads.at[1 - section], grads_all.at[place], pair_send.at[5], pair_recv.at[5], other))
    loads[1].wait()
    loads[3].wait()

    def block(p, stage):
        first, size = p * PART_ROWS, PART_ROWS
        for s in range(stage):
            size //= 4
            first = first + coords[(p + s) % 3] * size
        return first, size

    def spread(p, stage, source, got):
        axis = (p + stage) % 3
        size = PART_ROWS // 4 ** (stage + 1)
        sent = []
        for distance in (1, 2, 3):
            to = lax.rem(coords[axis] + distance, 4)
            i = (p * 3 + stage) * 3 + distance - 1
            sent.append(
                copy(
                    source.at[pl.ds(pl.multiple_of(to * size, size), size)],
                    got.at[p, distance - 1],
                    send.at[i],
                    recv.at[i],
                    peer(axis, distance),
                )
            )
        return sent

    def total(p, stage, source, got):
        size = PART_ROWS // 4 ** (stage + 1)
        kept = source[pl.ds(pl.multiple_of(coords[(p + stage) % 3] * size, size), size), :].astype(F32)
        for d in range(3):
            kept = kept + got[p, d].astype(F32)
        return kept

    small_waits = []

    def small_spread(stage, axis, source_of, dst_of):
        sent = []
        for distance in (1, 2, 3):
            i = stage * 3 + distance - 1
            to = lax.rem(coords[axis] + distance, 4)
            sent.append(copy(source_of(to), dst_of(distance), small_send.at[i], small_recv.at[i], peer(axis, distance)))
        return sent

    flights = {}
    for p in range(PARTS):
        pairs[p].wait()
        rows = at(p * PART_ROWS, PART_ROWS)
        own[rows, :] = (own[rows, :].astype(F32) + pair[rows, :].astype(F32)).astype(BF)
        flights[p] = spread(p, 0, own.at[rows], got1)
    pairs[3].wait()
    small_own[...] += small_pair[...]

    def quarter(index):
        return pl.ds(pl.multiple_of(index * 8, 8), 8)

    small_flight = small_spread(0, 0, lambda to: small_own.at[quarter(to)], lambda d: small_got.at[0, d - 1])

    for p in range(PARTS):
        for sent in flights[p]:
            sent.wait()
        rows = at(p * PART_ROWS, PART_ROWS)
        sum1[p] = total(p, 0, own.at[rows], got1).astype(BF)
        flights[p] = spread(p, 1, sum1.at[p], got2)
    for sent in small_flight:
        sent.wait()
    small_sum[0] = small_own[quarter(coords[0]), :] + small_got[0, 0] + small_got[0, 1] + small_got[0, 2]
    small_flight = small_spread(1, 1, lambda to: small_sum.at[0], lambda d: small_got.at[1, d - 1])
    for p in range(PARTS):
        for sent in flights[p]:
            sent.wait()
        sum2[p] = total(p, 1, sum1.at[p], got2).astype(BF)
        flights[p] = spread(p, 2, sum2.at[p], got3)
    for sent in small_flight:
        sent.wait()
    small_sum[1] = small_sum[0] + small_got[1, 0] + small_got[1, 1] + small_got[1, 2]
    small_flight = small_spread(2, 2, lambda to: small_sum.at[1], lambda d: small_got.at[2, d - 1])

    def gather(p, stage):
        axis = (p + stage) % 3
        first, size = block(p, stage + 1)
        rows = pl.ds(pl.multiple_of(first, size), size)
        sent = []
        for distance in (1, 2, 3):
            i = (p * 3 + stage) * 3 + distance - 1
            sent.append(copy(weight_all.at[rows], weight_all.at[rows], back_send.at[i], back_recv.at[i], peer(axis, distance)))
        return sent

    for p in range(PARTS):
        for sent in flights[p]:
            sent.wait()
        first, size = block(p, 3)
        weight_all[pl.ds(pl.multiple_of(first, size), size), :] = total(p, 2, sum2.at[p], got3).astype(BF)
        flights[p] = gather(p, 2)
    for sent in small_flight:
        sent.wait()
    small_all[quarter(coords[0]), :] = small_sum[1] + small_got[2, 0] + small_got[2, 1] + small_got[2, 2]
    small_flight = small_spread(
        3, 0, lambda to: small_all.at[quarter(coords[0])], lambda d: small_all.at[quarter(coords[0])]
    )
    for stage in (1, 0):
        for p in range(PARTS):
            for sent in flights[p]:
                sent.wait()
            flights[p] = gather(p, stage)
    for p in range(PARTS):
        for sent in flights[p]:
            sent.wait()
    for sent in small_flight:
        sent.wait()
    pairs[4].wait()
    pairs[5].wait()
    loads[4].wait()
    loads[5].wait()


def reduce(acts, grads, weight_grads, small_sums):
    vmem = pl.BlockSpec(memory_space=pltpu.VMEM)
    hbm = pl.BlockSpec(memory_space=pl.ANY)
    quarter = PART_ROWS // 4
    return pl.pallas_call(
        reduce_kernel,
        out_shape=[
            jax.ShapeDtypeStruct((2 * M, D), BF),
            jax.ShapeDtypeStruct((2 * M, D), BF),
            jax.ShapeDtypeStruct((GRADS, D), BF),
            jax.ShapeDtypeStruct((SMALL, D), F32),
        ],
        in_specs=[hbm] * 4,
        out_specs=[hbm, hbm, vmem, vmem],
        scratch_shapes=[
            pltpu.VMEM((GRADS, D), BF),
            pltpu.VMEM((GRADS, D), BF),
            pltpu.VMEM((GRADS, D), BF),
            pltpu.VMEM((PARTS, 3, quarter, D), BF),
            pltpu.VMEM((PARTS, 3, quarter // 4, D), BF),
            pltpu.VMEM((PARTS, 3, quarter // 16, D), BF),
            pltpu.VMEM((PARTS, quarter, D), BF),
            pltpu.VMEM((PARTS, quarter // 4, D), BF),
            pltpu.VMEM((SMALL, D), F32),
            pltpu.VMEM((SMALL, D), F32),
            pltpu.VMEM((SMALL, D), F32),
            pltpu.VMEM((3, 3, 8, D), F32),
            pltpu.VMEM((2, 8, D), F32),
            pltpu.SemaphoreType.DMA((6,)),
            pltpu.SemaphoreType.DMA((6,)),
            pltpu.SemaphoreType.DMA((6,)),
            pltpu.SemaphoreType.DMA((27,)),
            pltpu.SemaphoreType.DMA((27,)),
            pltpu.SemaphoreType.DMA((27,)),
            pltpu.SemaphoreType.DMA((27,)),
            pltpu.SemaphoreType.DMA((12,)),
            pltpu.SemaphoreType.DMA((12,)),
        ],
        compiler_params=pltpu.CompilerParams(collective_id=0, has_side_effects=True, vmem_limit_bytes=40 * MIB),
    )(acts, grads, weight_grads, small_sums)


def shards(
    frames, cotangent, lengths, bw_ids, conv_weight, conv_bias, scale_table, shift_table,
    w_up, b_up, w_down, b_down, layer_scale,
):
    own_small = jnp.concatenate(
        [conv_weight[0], conv_bias, scale_table[0], shift_table[0], b_down, layer_scale, b_up.reshape(3, D),
         jnp.zeros((24 - SMALL_ROWS, D), F32)]
    )
    swap = [(0, 1), (1, 0)]
    far_small = lax.ppermute(own_small, "section", swap)
    far_up = lax.ppermute(w_up[0], "section", swap)
    far_down = lax.ppermute(w_down[0], "section", swap)
    acts, grads, weight_grads, small_sums = compute(
        lengths, bw_ids, frames, cotangent, own_small, far_small, w_up[0], far_up, w_down[0], far_down
    )
    acts, grads, weights, small = reduce(acts, grads, weight_grads, small_sums)
    g_down = weights[:FF].astype(F32)
    g_up = jnp.concatenate([weights[FF + k * D : FF + (k + 1) * D] for k in range(3)], axis=1).astype(F32)
    return (
        acts[None],
        grads.astype(F32)[None],
        small[None, TAPS : TAPS + 7],
        small[CBIAS : CBIAS + 1],
        small[None, SCALE : SCALE + 4],
        small[None, SHIFT : SHIFT + 4],
        g_up[None],
        small[UBIAS : UBIAS + 3].reshape(1, FF),
        g_down[None],
        small[DBIAS : DBIAS + 1],
        small[GAMMA : GAMMA + 1],
    )


def solution(mesh):
    rows = P("dp", None)
    matrix, vector = P("section", None, None), P("section", None)
    in_specs = (rows,) * 4 + (matrix, vector, matrix, matrix, matrix, vector, matrix, vector, vector)
    stacked = P("section", "dp", None)
    out_specs = (stacked, stacked, matrix, vector, matrix, matrix, matrix, vector, matrix, vector, vector)
    return jax.shard_map(shards, mesh=mesh, in_specs=in_specs, out_specs=out_specs, check_vma=False)
```

time: 692 us -> 122 us (0.18)
  the two profiles are of different devices: /device:TPU:0 before, /device:TPU:2 now
where the time goes in v1:
time: 122 us; the launch traced here: 121 us
  Pallas kernels  98.7 us (81%)
  local copies, waits for them, and re-layouts  11.7 us (10%)
  other arithmetic  7.5 us (6%)
  waiting for transfers between devices  1.71 us (1%)
    pallas_call x1, Pallas kernels, reduce(): pl.pallas_call(reduce_kernel, out_shape=[jax.ShapeDtypeStruct((2 * M, D),...  58.2 us
    pallas_call x1, Pallas kernels, compute(): pl.pallas_call(compute_kernel, out_shape=[jax.ShapeDtypeStruct((2, M, D),...  40.5 us
    unnamed x17, local copies, waits for them, and re-layouts  8.22 us
    broadcast_in_dim x1, other arithmetic, shards(): grads.astype(F32)[None]  2.61 us
  transfers between devices with their start and end apart: 3, of which 2 were waited for; matrix products, arithmetic and copies ran while one was open for 3% of the time, Pallas kernels for 0%

profile of v1, /device:TPU:2, one launch (start us, length us, event | category | flops | bytes accessed | tf_op | source)
XLA Modules:
  0.0 121.1 jit_solution(11723385161941786910)
XLA Ops:
  0.6 0.1 collective-permute-start.1
  0.7 0.5 collective-permute-start.2
  1.2 0.7 reduce
  2.0 0.7 copy.28
  2.7 2.1 %concatenate.19.own_small = f32[24,512]{1,0:T(8,128)S(1)} concatenate(f32[7,512]{1,0:T(8,128)S(1)} %bitcast.31, f32[1,512]{1,0:T(1,128)} %param.18, f32[4,512]{1,0:T(4,128)} %bitcast.32, f32[4,512]{1,0:T(4,128)} %bitcast.33, f32[1,512]{1,0:T(1,128)} %param.24, f32[1,512]{1,0:T(1,128)} %param.25, f32[3,512]{1,0:T(4,128)S(1)} %reshape.70, f32[3,512]{1,0:T(4,128)S(1)} %broadcast_in_dim.28), dimensions={0} | concatenate | bytes 98304 | tf_op jit(solution)/shard_map/concatenate | solution.py:566
  4.8 0.0 copy-start.3
  4.8 0.2 collective-permute-start
  5.0 1.4 %collective-permute-done.far_small = f32[24,512]{1,0:T(8,128)S(1)} collective-permute-done((f32[24,512]{1,0:T(8,128)S(1)}, f32[24,512]{1,0:T(8,128)S(1)}, u32[]{:S(2)}, u32[]{:S(2)}) %collective-permute-start) | collective-permute-done | bytes 49184 | tf_op jit(solution)/shard_map/ppermute | solution.py:571
  6.5 0.0 copy-start.5
  6.5 0.0 collective-permute-done.1.far_up
  6.5 0.0 copy-start.4
  6.5 0.3 collective-permute-done.2.far_down
  6.7 0.0 copy-done.3
  6.7 0.3 copy-done.5
  7.1 0.5 copy-done.4
  7.6 40.5 %shard_map.212 = (bf16[2,1024,512]{2,1,0:T(8,128)(2,1)}, bf16[2,1024,512]{2,1,0:T(8,128)(2,1)}, bf16[2,3072,512]{2,1,0:T(8,128)(2,1)}, f32[2,32,512]{2,1,0:T(8,128)}) custom-call(s32[4,4]{1,0:T(4,128)} %lengths.1, s32[4,4]{1,0:T(4,128)} %ids.1, bf16[2048,512]{1,0:T(8,128)(2,1)} %frames.1, bf16[2048,512]{1,0:T(8,128)(2,1)} %cotangent.1, f32[24,512]{1,0:T(8,128)} %copy-done.3, ...), custom_call_target="tpu_custom_call" | custom-call | flops 19327352832 | bytes 25165824 | tf_op jit(solution)/shard_map/pallas_call | solution.py:299
  48.1 0.0 copy-start
  48.1 1.6 %copy-done = bf16[2,1024,512]{2,1,0:T(8,128)(2,1)S(1)} copy-done((bf16[2,1024,512]{2,1,0:T(8,128)(2,1)S(1)}, bf16[2,1024,512]{2,1,0:T(8,128)(2,1)}, u32[]{:S(2)}) %copy-start) | copy-done | bytes 2097176
  49.7 0.0 copy-start.1
  49.7 1.6 %copy-done.1 = bf16[2,1024,512]{2,1,0:T(8,128)(2,1)S(1)} copy-done((bf16[2,1024,512]{2,1,0:T(8,128)(2,1)S(1)}, bf16[2,1024,512]{2,1,0:T(8,128)(2,1)}, u32[]{:S(2)}) %copy-start.1) | copy-done | bytes 2097176
  51.3 0.0 copy-start.2
  51.3 0.9 copy-done.2
  52.2 58.2 %shard_map.213 = (bf16[2048,512]{1,0:T(8,128)(2,1)S(1)}, bf16[2048,512]{1,0:T(8,128)(2,1)S(1)}, bf16[3072,512]{1,0:T(8,128)(2,1)S(1)}, f32[32,512]{1,0:T(8,128)S(1)}) custom-call(bf16[2,1024,512]{2,1,0:T(8,128)(2,1)S(1)} %copy-done, bf16[2,1024,512]{2,1,0:T(8,128)(2,1)S(1)} %copy-done.1, bf16[2,3072,512]{2,1,0:T(8,128)(2,1)} %get-tuple-element.21.weight_grads, ...), custom_call_target="tpu_custom_call" | custom-call | tf_op jit(solution)/shard_map/pallas_call | solution.py:524
  110.4 0.6 fusion
  111.0 0.6 slice_bitcast_fusion.5
  111.6 0.1 slice_bitcast_fusion.2
  111.7 2.1 %bitcast_convert_fusion.1 = f32[1,1536,512]{2,1,0:T(8,128)} fusion(bf16[3072,512]{1,0:T(8,128)(2,1)S(1)} %get-tuple-element.26), kind=kLoop, calls=%fused_computation.2 | loop fusion | flops 786432 | bytes 4718592 | tf_op jit(solution)/shard_map/broadcast_in_dim | solution.py:589
  113.9 0.6 copy.26
  114.5 0.6 copy.24
  115.1 2.6 %bitcast_convert_fusion = f32[1,2048,512]{2,1,0:T(8,128)} fusion(bf16[2048,512]{1,0:T(8,128)(2,1)S(1)} %get-tuple-element.24), kind=kLoop, calls=%fused_computation | loop fusion | flops 1048576 | bytes 6291456 | tf_op jit(solution)/shard_map/broadcast_in_dim | solution.py:582
  117.7 2.1 %maximum_convert_fusion = f32[1,512,1536]{2,1,0:T(8,128)} fusion(bf16[1,512,512]{2,1,0:T(8,128)(2,1)S(1)} %get-tuple-element.39, bf16[1,512,512]{2,1,0:T(8,128)(2,1)S(1)} %get-tuple-element.40, bf16[1,512,512]{2,1,0:T(8,128)(2,1)S(1)} %get-tuple-element.38), kind=kLoop, calls=%fused_computation.1 | loop fusion | flops 4718592 | bytes 4718592 | tf_op jit(solution)/shard_map/convert_element_type | solution.py:579
  119.8 1.3 %copy.30 = bf16[1,2048,512]{2,1,0:T(8,128)(2,1)} copy(bf16[1,2048,512]{2,1,0:T(8,128)(2,1)S(1)} %bitcast.30) | data formatting | bytes 4194304
  (4 shorter events, 0.0 us)
Async XLA Ops:
  0.6 5.8 %collective-permute-start.1 = (bf16[512,1536]{1,0:T(8,128)(2,1)}, bf16[512,1536]{1,0:T(8,128)(2,1)S(1)}, u32[]{:S(2)}, u32[]{:S(2)}) collective-permute-start(bf16[512,1536]{1,0:T(8,128)(2,1)} %bitcast.35), channel_id=1, source_target_pairs={{0,64},{64,0},{1,65},{65,1},{2,66},{66,2},{3,67},{67,3},{4,68},{68... | collective-permute-start | bytes 4718600 | tf_op jit(solution)/shard_map/ppermute | solution.py:572
  0.7 6.0 %collective-permute-start.2 = (bf16[1536,512]{1,0:T(8,128)(2,1)}, bf16[1536,512]{1,0:T(8,128)(2,1)}, u32[]{:S(2)}, u32[]{:S(2)}) collective-permute-start(bf16[1536,512]{1,0:T(8,128)(2,1)} %bitcast.37), channel_id=1, source_target_pairs={{0,64},{64,0},{1,65},{65,1},{2,66},{66,2},{3,67},{67,3},{4,68},{68... | collective-permute-start | bytes 4718600 | tf_op jit(solution)/shard_map/ppermute | solution.py:573
  4.8 1.9 %copy-start.3 = (f32[24,512]{1,0:T(8,128)}, f32[24,512]{1,0:T(8,128)S(1)}, u32[]{:S(2)}) copy-start(f32[24,512]{1,0:T(8,128)S(1)} %concatenate.19.own_small) | copy-start | bytes 147460
  4.8 1.6 %collective-permute-start = (f32[24,512]{1,0:T(8,128)S(1)}, f32[24,512]{1,0:T(8,128)S(1)}, u32[]{:S(2)}, u32[]{:S(2)}) collective-permute-start(f32[24,512]{1,0:T(8,128)S(1)} %concatenate.19.own_small), channel_id=1, source_target_pairs={{0,64},{64,0},{1,65},{65,1},{2,66},{66,2},{3,67},{67,3},{4,68},{68... | collective-permute-start | bytes 147464 | tf_op jit(solution)/shard_map/ppermute | solution.py:571
  6.5 0.6 copy-start.5
  6.5 1.2 copy-start.4
  48.1 1.6 %copy-start = (bf16[2,1024,512]{2,1,0:T(8,128)(2,1)S(1)}, bf16[2,1024,512]{2,1,0:T(8,128)(2,1)}, u32[]{:S(2)}) copy-start(bf16[2,1024,512]{2,1,0:T(8,128)(2,1)} %get-tuple-element.19.acts) | copy-start | bytes 6291460
  49.7 1.6 %copy-start.1 = (bf16[2,1024,512]{2,1,0:T(8,128)(2,1)S(1)}, bf16[2,1024,512]{2,1,0:T(8,128)(2,1)}, u32[]{:S(2)}) copy-start(bf16[2,1024,512]{2,1,0:T(8,128)(2,1)} %get-tuple-element.20.grads) | copy-start | bytes 6291460
  51.3 0.9 copy-start.2
